TPU v7x, 32 devices: a whole 2x2x4 slice. The times are simulated.
32 devices in a mesh: grp: 4 (over z), pair: 8 (over y, x, core).
Axes of the slice: x: 2, y: 2, z: 4, core: 2. Of those that a mesh axis runs over, the one named last changes fastest.
Arguments:
- three_center: bfloat16 [512, 1024, 1024], P('pair', 'grp'), may hold values from -6 to 6
- virt_density: bfloat16 [1024, 1024], P(None, 'pair'), may hold values from -0.1875 to 0.1875
- occ_density: bfloat16 [1024, 1024], P(None, 'pair'), may hold values from -0.1875 to 0.1875
- tensor_mask: int32 [4, 8, 8], replicated, may hold values 0 or 1
- virt_mask: int32 [8, 8], replicated, may hold values 0 or 1
- occ_mask: int32 [8, 8], replicated, may hold values 0 or 1
- panel_order: int32 [512], replicated, may hold values from 0 to 511, each once
Outputs:
- response: float32 [512, 512], P(('grp', 'pair'))
Inputs may be any that keep to these rules, and one draw needn't show every extreme that they name: `tensor_mask`: each block is 0 (absent) or 1 (present). `virt_mask`: each block is 0 (absent) or 1 (present). `occ_mask`: each block is 0 (absent) or 1 (present). `panel_order`: every auxiliary index appears exactly once.
All inputs are finite; a program needn't handle non-finite values.
Results may differ from a plain program's by a relative error of at most 0.0041.
Values may be sent and summed in bfloat16 or wider, within the bound.
A program may use at most 256 MiB of HBM per device.

v0:
```python
import jax
import jax.numpy as jnp
from jax import lax
from jax.sharding import PartitionSpec as P

NORB = 1024
BLK = 128


def spread_blocks(table):
    return jnp.repeat(jnp.repeat(table, BLK, axis=0), BLK, axis=1)


def density_local(density, mask_table, offset):
    full_mask = spread_blocks(mask_table).astype(jnp.bfloat16)
    local_mask = lax.dynamic_slice_in_dim(full_mask, offset, density.shape[1], 1)
    return density * local_mask


def per_device(
    three_center, virt_density, occ_density, tensor_mask, virt_mask, occ_mask, panel_order
):
    slab_rows, section_rows, orbitals = three_center.shape
    column_count = virt_density.shape[1]
    column_start = lax.axis_index("pair") * column_count
    aux_start = lax.axis_index("pair") * slab_rows
    row_block = (aux_start + jnp.arange(slab_rows, dtype=jnp.int32)) // BLK
    block_ids = jnp.arange(tensor_mask.shape[0], dtype=jnp.int32)
    selector = (row_block[:, None] == block_ids[None, :]).astype(jnp.float32)
    block_start = lax.axis_index("grp") * (section_rows // BLK)
    sub_mask = lax.dynamic_slice_in_dim(tensor_mask, block_start, section_rows // BLK, 1).astype(
        jnp.float32
    )
    row_mask = jnp.einsum("ab,bmn->amn", selector, sub_mask)
    row_mask = jnp.repeat(jnp.repeat(row_mask, BLK, axis=1), BLK, axis=2).astype(jnp.bfloat16)
    masked = three_center * row_mask
    virt_local = density_local(virt_density, virt_mask, column_start)
    occ_local = density_local(occ_density, occ_mask, column_start)
    half = jnp.einsum(
        "amn,ns->ams",
        masked,
        lax.all_gather(virt_local, "pair", axis=1, tiled=True),
        preferred_element_type=jnp.float32,
    ).astype(jnp.bfloat16)
    swapped = lax.all_to_all(half, "grp", split_axis=2, concat_axis=1, tiled=True)
    trans = jnp.einsum(
        "ams,ml->asl",
        swapped,
        lax.all_gather(occ_local, "pair", axis=1, tiled=True),
        preferred_element_type=jnp.float32,
    ).astype(jnp.bfloat16)
    owned_trans, owned_tensor = (
        lax.all_to_all(trans, "pair", split_axis=2, concat_axis=0, tiled=True),
        lax.all_to_all(masked, "pair", split_axis=2, concat_axis=0, tiled=True),
    )
    owned_trans = owned_trans.reshape(owned_trans.shape[0], -1)
    owned_tensor = owned_tensor.reshape(owned_tensor.shape[0], -1)
    picked_all = jnp.take(owned_trans, panel_order, axis=0)
    product_all = lax.dot_general(
        picked_all, owned_tensor, (((1,), (1,)), ((), ())), preferred_element_type=jnp.float32
    )
    product_all = product_all * (1.0 / NORB)
    return lax.psum_scatter(product_all, ("grp", "pair"), scatter_dimension=0, tiled=True)


def solution(mesh):
    placed = (P("pair", "grp", None), P(None, "pair"), P(None, "pair"), P(), P(), P(), P())
    return jax.shard_map(
        per_device, mesh=mesh, in_specs=placed, out_specs=P(("grp", "pair"), None), check_vma=False
    )
```

profile of v0, /device:TPU:0, one launch (start us, length us, event | category | flops | bytes accessed | tf_op | source)
XLA Modules:
  0.0 2009.5 jit_solution(11984036613436026233)
XLA Ops:
  6.5 0.7 convert_element_type.47
  7.3 2.9 broadcast_in_dim.36
  10.2 0.6 copy.50
  10.9 1.8 dynamic-slice_multiply_fusion.1
  12.7 0.2 convolution_convert_fusion.1
  12.9 0.2 copy.18
  13.1 0.6 broadcast_in_dim.33
  13.7 0.2 convert_element_type.45
  13.9 45.4 %copy.19 = bf16[64,256,1024]{1,0,2:T(8,128)(2,1)} copy(bf16[64,256,1024]{2,1,0:T(8,128)(2,1)} %param.7) | data formatting | bytes 67108864 | tf_op args[0]
  59.2 23.4 %bitcast_multiply_fusion = bf16[64,256,1024]{1,0,2:T(8,128)(2,1)} fusion(bf16[64,256,1024]{1,0,2:T(8,128)(2,1)} %copy.19, bf16[64,256,8]{1,0,2:T(8,128)(2,1)S(1)} %convert_element_type.45), kind=kLoop, calls=%fused_computation.5 | loop fusion | flops 16777216 | bytes 67371008 | tf_op jit(solution)/shard_map/mul | solution.py:36
  82.6 61.5 %fusion.7 = bf16[64,256,1024]{2,1,0:T(8,128)(2,1)} fusion(bf16[64,256,1024]{1,0,2:T(8,128)(2,1)} %bitcast_multiply_fusion, bf16[1024,1024]{1,0:T(8,128)(2,1)} %all-gather.3.cloned.1.call-done), kind=kOutput, calls=%fused_computation.11 | convolution fusion | flops 34376515584 | bytes 69206016 | tf_op jit(solution)/shard_map/amn,ns->ams/dot_general | solution.py:39
  144.1 45.2 %copy.21 = bf16[64,256,1024]{1,0,2:T(8,128)(2,1)} copy(bf16[64,256,1024]{2,1,0:T(8,128)(2,1)} %fusion.7) | data formatting | bytes 67108864 | tf_op jit(solution)/shard_map/convert_element_type | solution.py:44
  189.3 742.3 %all_to_all.48 = bf16[64,256,1024]{1,0,2:T(8,128)(2,1)} all-to-all(bf16[64,256,1024]{1,0,2:T(8,128)(2,1)} %copy.21), channel_id=1, replica_groups=mesh['grp'=4,'pair'=8] {'grp'}, dimensions={2} | all-to-all | bytes 67108864 | tf_op jit(solution)/shard_map/all_to_all | solution.py:45
  931.6 7.3 all-to-all-start.2
  939.1 2.9 broadcast_in_dim.38
  942.0 0.6 copy.49
  942.6 0.8 dynamic-slice_multiply_fusion
  943.5 42.4 %copy.48 = bf16[64,256,4,256]{1,2,3,0:T(4,128)(2,1)} copy(bf16[64,256,4,256]{1,0,3,2:T(8,128)(2,1)} %bitcast.47) | data formatting | bytes 67108864 | tf_op jit(solution)/shard_map/all_to_all | solution.py:45
  985.9 53.7 %all_to_all.38 = bf16[64,1024,256]{1,2,0:T(8,128)(2,1)} reshape(bf16[64,4,256,256]{2,1,3,0:T(4,128)(2,1)} %bitcast.48) | data formatting | bytes 67108864 | tf_op jit(solution)/shard_map/all_to_all | solution.py:45
  1039.5 99.4 %all-gather.5.cloned.1.call-done = bf16[1024,1024]{1,0:T(8,128)(2,1)} async-done(((bf16[1024,128]{1,0:T(8,128)(2,1)}), bf16[1024,1024]{1,0:T(8,128)(2,1)}) %all-gather.5.cloned.1.call-update) | async-done | bytes 2097168 | tf_op jit(solution)/shard_map/all_gather | solution.py:49
  1139.0 42.9 %convolution_convert_fusion = bf16[64,256,1024]{2,1,0:T(8,128)(2,1)} fusion(bf16[64,1024,256]{1,2,0:T(8,128)(2,1)} %all_to_all.38, bf16[1024,1024]{1,0:T(8,128)(2,1)} %all-gather.5.cloned.1.call-done), kind=kOutput, calls=%fused_computation.12 | convolution fusion | flops 34376515584 | bytes 69206016 | tf_op jit(solution)/shard_map/ams,ml->asl/dot_general | solution.py:46
  1181.9 45.4 %copy.23 = bf16[64,256,1024]{1,0,2:T(8,128)(2,1)} copy(bf16[64,256,1024]{2,1,0:T(8,128)(2,1)} %convolution_convert_fusion) | data formatting | bytes 67108864 | tf_op jit(solution)/shard_map/convert_element_type | solution.py:51
  1227.3 83.8 %all-to-all-done.2 = bf16[64,256,1024]{1,0,2:T(8,128)(2,1)} async-done(((bf16[64,256,1024]{1,0,2:T(8,128)(2,1)}), bf16[64,256,1024]{1,0,2:T(8,128)(2,1)}, u32[]{:S(2)}, u32[]{:S(2)}) %all-to-all-start.2) | async-done | bytes 33554464 | tf_op jit(solution)/shard_map/all_to_all | solution.py:54
  1311.1 7.1 all-to-all-start.1
  1318.2 0.0 reduce-scatter.2.cloned.1.call-start
  1318.3 45.2 %copy.25 = bf16[64,256,8,128]{3,1,0,2:T(8,128)(2,1)} copy(bf16[64,256,8,128]{1,0,3,2:T(8,128)(2,1)} %bitcast.10) | data formatting | bytes 67108864 | tf_op jit(solution)/shard_map/all_to_all | solution.py:54
  1363.5 318.4 %all-to-all-done.1 = bf16[64,256,1024]{1,0,2:T(8,128)(2,1)} async-done(((bf16[64,256,1024]{1,0,2:T(8,128)(2,1)}), bf16[64,256,1024]{1,0,2:T(8,128)(2,1)}, u32[]{:S(2)}, u32[]{:S(2)}) %all-to-all-start.1) | async-done | bytes 33554464 | tf_op jit(solution)/shard_map/all_to_all | solution.py:53
  1681.9 45.2 %copy.24 = bf16[64,256,8,128]{3,1,0,2:T(8,128)(2,1)} copy(bf16[64,256,8,128]{1,0,3,2:T(8,128)(2,1)} %bitcast.8) | data formatting | bytes 67108864 | tf_op jit(solution)/shard_map/all_to_all | solution.py:53
  1727.1 30.3 %copy.47 = bf16[64,8,256,128]{3,1,2,0:T(8,128)(2,1)} copy(bf16[64,8,256,128]{3,2,1,0:T(8,128)(2,1)} %bitcast.49) | data formatting | bytes 67108864
  1757.4 66.0 %gather_fusion = bf16[512,32768]{1,0:T(8,128)(2,1)} fusion(bf16[512,32768]{1,0:T(8,128)(2,1)} %bitcast.46, s32[1024]{0:T(1024)S(1)} %pad_clamp_fusion), kind=kCustom, calls=%fused_computation | custom fusion | bytes 67110912 | tf_op jit(solution)/shard_map/jit(_take)/gather | solution.py:58
  1823.4 47.1 %fusion.13 = f32[512,512]{1,0:T(8,128)} fusion(bf16[64,8,256,128]{3,2,1,0:T(8,128)(2,1)} %bitcast.50, bf16[512,32768]{1,0:T(8,128)(2,1)} %gather_fusion, pred[512]{0:T(512)(128)(4,1)S(1)} %compare_and_fusion), kind=kOutput, calls=%fused_computation.18 | convolution fusion | flops 17196908544 | bytes 68157952 | tf_op jit(solution)/shard_map/dot_general | solution.py:59
  1870.5 132.2 %reduce-scatter.2.cloned.1.call-done = f32[16,512]{1,0:T(8,128)} async-done(((f32[512,512]{1,0:T(8,128)}), f32[16,512]{1,0:T(8,128)}) %reduce-scatter.2.cloned.1.call-update) | async-done | bytes 32784 | tf_op jit(solution)/shard_map/reduce_scatter | solution.py:63
  (24 shorter events, 0.2 us)
Async XLA Ops:
  6.5 6.1 copy-start
  6.5 76.1 %all-gather.3.cloned.1.call-start = ((), (), s32[]{:S(2)}) async-start(), calls=%async_computation.4 | async-start | bytes 2359296 | tf_op jit(solution)/shard_map/all_gather | solution.py:42
  931.6 7.4 copy-start.4
  931.6 11.0 copy-start.2
  931.6 379.5 %all-to-all-start.2 = ((bf16[64,256,1024]{1,0,2:T(8,128)(2,1)}), bf16[64,256,1024]{1,0,2:T(8,128)(2,1)}, u32[]{:S(2)}, u32[]{:S(2)}) async-start(bf16[64,256,1024]{1,0,2:T(8,128)(2,1)} %bitcast_multiply_fusion), calls=%async_computation.2 | async-start | bytes 67108864 | tf_op jit(solution)/shard_map/all_to_all | solution.py:54
  938.9 200.0 %all-gather.5.cloned.1.call-start = ((), (), s32[]{:S(2)}) async-start(), calls=%async_computation.5 | async-start | bytes 2359296 | tf_op jit(solution)/shard_map/all_gather | solution.py:49
  1227.3 90.9 %copy-start.3 = (s32[512]{0:T(512)S(1)}, s32[512]{0:T(512)}, u32[]{:S(2)}) copy-start(s32[512]{0:T(512)} %param.13) | copy-start | bytes 6148
  1311.1 370.8 %all-to-all-start.1 = ((bf16[64,256,1024]{1,0,2:T(8,128)(2,1)}), bf16[64,256,1024]{1,0,2:T(8,128)(2,1)}, u32[]{:S(2)}, u32[]{:S(2)}) async-start(bf16[64,256,1024]{1,0,2:T(8,128)(2,1)} %copy.23), calls=%async_computation.1 | async-start | bytes 67108864 | tf_op jit(solution)/shard_map/all_to_all | solution.py:53
  1318.2 684.5 %reduce-scatter.2.cloned.1.call-start = ((), (), s32[]{:S(2)}) async-start(), calls=%async_computation.6 | async-start | bytes 1081344 | tf_op jit(solution)/shard_map/reduce_scatter | solution.py:63
  1823.4 179.4 %copy-start.1 = (s32[4,8,8]{2,1,0:T(8,128)S(1)}, s32[4,8,8]{2,1,0:T(8,128)}, u32[]{:S(2)}) copy-start(s32[4,8,8]{2,1,0:T(8,128)} %param.10) | copy-start | bytes 3076
Sparse Core Ops, SparseCore 0:
  12.8 30.8 all-gather.2
  943.6 195.3 all-gather.4
  1870.6 132.0 reduce-scatter.1
where the time goes:
time: 2020 us; the launch traced here: 2010 us
  blocking collectives  742 us (37%)
  waiting for transfers between devices  634 us (31%)
  local copies, waits for them, and re-layouts  427 us (21%)
  matrix products  152 us (8%)
  other arithmetic  26.7 us (1%)
    all_to_all x1, blocking collectives, per_device(): lax.all_to_all(half, 'grp', split_axis=2, concat_axis=1, tiled=True)  742 us
    all_to_all x1, waiting for transfers between devices, per_device(): lax.all_to_all(trans, 'pair', split_axis=2, concat_axis=0, tiled=True)  318 us
    reduce_scatter x1, waiting for transfers between devices, per_device(): lax.psum_scatter(product_all, ('grp', 'pair'), scatter_dimension=0, tiled...  132 us
    all_gather x1, waiting for transfers between devices, per_device(): lax.all_gather(occ_local, 'pair', axis=1, tiled=True)  99.4 us
    all_to_all x2, local copies, waits for them, and re-layouts, per_device(): lax.all_to_all(half, 'grp', split_axis=2, concat_axis=1, tiled=True)  96 us
    all_to_all x1, waiting for transfers between devices, per_device(): lax.all_to_all(masked, 'pair', split_axis=2, concat_axis=0, tiled=True)  83.8 us
    unnamed x14, local copies, waits for them, and re-layouts  76.9 us
    gather x1, local copies, waits for them, and re-layouts, per_device(): picked_all = jnp.take(owned_trans, panel_order, axis=0)  66 us
  transfers between devices with their start and end apart: 5, of which 4 were waited for; matrix products, arithmetic and copies ran while one was open for 12% of the time, Pallas kernels for 0%

commit v1 on v0

v1 whole, which is shorter than its diff:
```python
import functools

import jax
import jax.numpy as jnp
from jax import lax
from jax.experimental import pallas as pl
from jax.experimental.pallas import tpu as pltpu
from jax.sharding import PartitionSpec as P

LANES = 128
MESH = pl.DeviceIdType.MESH
MIB = 1024 * 1024


def enter(grp, pair):
    g, p = lax.axis_index("grp"), lax.axis_index("pair")
    barrier = pltpu.get_barrier_semaphore()

    def greet(k, carry):
        there = lax.rem(g * pair + p + k, grp * pair)
        pl.semaphore_signal(
            barrier, inc=1, device_id=(there // pair, lax.rem(there, pair)), device_id_type=MESH
        )
        return carry

    lax.fori_loop(1, grp * pair, greet, 0)
    pl.semaphore_wait(barrier, grp * pair - 1)


def exchange_kernel(
    grp, pair, slots,
    tensor, virt_own, occ_own, mask,
    half_all, turn_all,
    tensor_buf, virt, occ, wide, half_buf, turn_buf,
    load_sem, half_send, turn_send, half_recv, turn_recv, dens_send, dens_recv,
):
    g, p = lax.axis_index("grp"), lax.axis_index("pair")
    slab, width, orbitals = tensor.shape
    chunk = tensor_buf.shape[1]
    chunks = slab // chunk
    rows = width // pair
    cols = virt_own.shape[0]
    blocks = mask.shape[1]
    edge = width // blocks
    steps = chunks * grp

    def load(c):
        return pltpu.make_async_copy(
            tensor.at[pl.ds(c * chunk, chunk)], tensor_buf.at[lax.rem(c, 2)],
            load_sem.at[lax.rem(c, 2)],
        )

    load(0).start()
    enter(grp, pair)

    def density(which, k):
        own, full = ((virt_own, virt), (occ_own, occ))[which]
        return pltpu.make_async_remote_copy(
            src_ref=own,
            dst_ref=full.at[pl.ds(pl.multiple_of(p * cols, cols), cols)],
            send_sem=dens_send.at[which, k],
            recv_sem=dens_recv.at[which, p],
            device_id=(g, lax.rem(p + k, pair)),
            device_id_type=MESH,
        )

    def density_arrived(which):
        full = (virt, occ)[which]
        for k in range(1, pair):
            sender = lax.rem(p + k, pair)
            part = full.at[pl.ds(pl.multiple_of(sender * cols, cols), cols)]
            pltpu.make_async_remote_copy(
                src_ref=part, dst_ref=part, send_sem=dens_send.at[which, k],
                recv_sem=dens_recv.at[which, sender],
                device_id=(g, sender), device_id_type=MESH,
            ).wait_recv()

    for which in range(2):
        for k in range(1, pair):
            density(which, k).start()
    own_rows = pl.ds(pl.multiple_of(p * cols, cols), cols)
    virt[own_rows, :] = virt_own[...]
    occ[own_rows, :] = occ_own[...]
    density_arrived(0)

    def place(buf, slot):
        def one(s, carry):
            for t in range(width // LANES):
                picked = wide[t, pl.ds(s, chunk, stride=width), :]
                buf[slot, s, :, t * LANES:(t + 1) * LANES] = picked.astype(buf.dtype)
            return carry

        lax.fori_loop(0, width, one, 0, unroll=8)

    def keep(i, product):
        for t in range(width // LANES):
            wide[t, pl.ds(pl.multiple_of(i * width, width), width), :] = (
                product[:, t * LANES:(t + 1) * LANES]
            )

    def wait_sent(buf, sems, slot):
        for k in range(pair):
            part = buf.at[slot, pl.ds(0, rows)]
            pltpu.make_async_copy(part, part, sems.at[slot, k]).wait()

    def send(buf, sends, slot, k, target_grp, dst, recv):
        target = lax.rem(p + k, pair)
        return pltpu.make_async_remote_copy(
            src_ref=buf.at[slot, pl.ds(target * rows, rows)], dst_ref=dst,
            send_sem=sends.at[slot, k], recv_sem=recv,
            device_id=(target_grp, target), device_id_type=MESH,
        )

    def stay(buf, sends, slot, dst):
        return pltpu.make_async_copy(
            buf.at[slot, pl.ds(p * rows, rows)], dst, sends.at[slot, 0]
        )

    def step(t, carry):
        c, u = t // grp, lax.rem(t, grp)
        b = lax.rem(c, 2)
        slot = lax.rem(t, slots)

        @pl.when(u == 0)
        def _():
            load(c).wait()

            @pl.when(c + 1 < chunks)
            def _():
                load(c + 1).start()

            def apply(i, carry):
                for block in range(blocks):
                    row = mask[c * chunk + i, block:block + 1, :]
                    row = jnp.broadcast_to(row, (16, orbitals)).astype(tensor_buf.dtype)
                    at = slice(block * edge, (block + 1) * edge)
                    part = tensor_buf[b, i, at, :].reshape(edge // 16, 16, orbitals)
                    tensor_buf[b, i, at, :] = (part * row[None]).reshape(edge, orbitals)
                return carry

            lax.fori_loop(0, chunk, apply, 0)

        @pl.when(t >= slots)
        def _():
            wait_sent(half_buf, half_send, slot)

        target_grp = lax.rem(g + 1 + u, grp)
        aux_rows = pl.ds(pl.multiple_of(p * slab + c * chunk, chunk), chunk)

        def half_one(i, carry):
            left = virt[pl.ds(pl.multiple_of(target_grp * width, width), width), :]
            keep(i, lax.dot_general(
                left, tensor_buf[b, i], (((1,), (1,)), ((), ())),
                preferred_element_type=jnp.float32,
            ))
            return carry

        lax.fori_loop(0, chunk, half_one, 0)
        place(half_buf, slot)
        dst = half_all.at[:, aux_rows, pl.ds(pl.multiple_of(g * width, width), width)]
        recv = half_recv.at[g * pair + p]

        @pl.when(target_grp == g)
        def _():
            stay(half_buf, half_send, slot, dst).start()

        @pl.when(target_grp != g)
        def _():
            send(half_buf, half_send, slot, 0, target_grp, dst, recv).start()

        for k in range(1, pair):
            send(half_buf, half_send, slot, k, target_grp, dst, recv).start()

        @pl.when(t == 0)
        def _():
            density_arrived(1)

        @pl.when(t >= slots)
        def _():
            wait_sent(turn_buf, turn_send, slot)

        section = pl.ds(pl.multiple_of(u * width, width), width)

        def turn_one(i, carry):
            keep(i, jnp.dot(
                tensor_buf[b, i], occ[:, section], preferred_element_type=jnp.float32
            ))
            return carry

        lax.fori_loop(0, chunk, turn_one, 0)
        place(turn_buf, slot)
        dst = turn_all.at[:, aux_rows, section]
        stay(turn_buf, turn_send, slot, dst).start()
        for k in range(1, pair):
            send(turn_buf, turn_send, slot, k, g, dst, turn_recv.at[p]).start()
        return carry

    lax.fori_loop(0, steps, step, 0)

    for t in range(max(steps - slots, 0), steps):
        wait_sent(half_buf, half_send, t % slots)
        wait_sent(turn_buf, turn_send, t % slots)
    for which in range(2):
        for k in range(1, pair):
            density(which, k).wait_send()

    def half_arrived(k, carry):
        sender = lax.rem(g * pair + p + k, grp * pair)
        sender_grp, sender_pair = sender // pair, lax.rem(sender, pair)
        part = half_all.at[
            :, pl.ds(pl.multiple_of(sender_pair * slab, slab), slab),
            pl.ds(pl.multiple_of(sender_grp * width, width), width),
        ]
        pltpu.make_async_remote_copy(
            src_ref=part, dst_ref=part, send_sem=half_send.at[0, 0],
            recv_sem=half_recv.at[sender],
            device_id=(sender_grp, sender_pair), device_id_type=MESH,
        ).wait_recv()
        return carry

    lax.fori_loop(1, grp * pair, half_arrived, 0)

    def turn_arrived(k, carry):
        sender = lax.rem(p + k, pair)
        part = turn_all.at[:, pl.ds(pl.multiple_of(sender * slab, slab), slab), :]
        pltpu.make_async_remote_copy(
            src_ref=part, dst_ref=part, send_sem=turn_send.at[0, 0],
            recv_sem=turn_recv.at[sender],
            device_id=(g, sender), device_id_type=MESH,
        ).wait_recv()
        return carry

    lax.fori_loop(1, pair, turn_arrived, 0)


def exchange(grp, pair, tensor, virt_own, occ_own, mask):
    slab, width, orbitals = tensor.shape
    chunk = 16
    slots = min(4, slab // chunk * grp)
    gathered = jax.ShapeDtypeStruct((width // pair, slab * pair, orbitals), tensor.dtype)
    flops = 4 * slab * width * orbitals * orbitals
    return pl.pallas_call(
        functools.partial(exchange_kernel, grp, pair, slots),
        out_shape=(gathered, gathered),
        in_specs=[pl.BlockSpec(memory_space=pl.ANY)]
        + [pl.BlockSpec(memory_space=pltpu.VMEM)] * 3,
        out_specs=(pl.BlockSpec(memory_space=pl.ANY),) * 2,
        scratch_shapes=[
            pltpu.VMEM((2, chunk, width, orbitals), tensor.dtype),
            pltpu.VMEM((orbitals, orbitals), tensor.dtype),
            pltpu.VMEM((orbitals, orbitals), tensor.dtype),
            pltpu.VMEM((width // LANES, chunk * width, LANES), jnp.float32),
            pltpu.VMEM((slots, width, chunk, width), tensor.dtype),
            pltpu.VMEM((slots, width, chunk, width), tensor.dtype),
            pltpu.SemaphoreType.DMA((2,)),
            pltpu.SemaphoreType.DMA((slots, pair)),
            pltpu.SemaphoreType.DMA((slots, pair)),
            pltpu.SemaphoreType.DMA((grp * pair,)),
            pltpu.SemaphoreType.DMA((pair,)),
            pltpu.SemaphoreType.DMA((2, pair)),
            pltpu.SemaphoreType.DMA((2, pair)),
        ],
        compiler_params=pltpu.CompilerParams(
            collective_id=0, has_side_effects=True, vmem_limit_bytes=56 * MIB
        ),
        cost_estimate=pl.CostEstimate(
            flops=flops, bytes_accessed=6 * slab * width * orbitals, transcendentals=0
        ),
    )(tensor, virt_own, occ_own, mask)


def product_kernel(scale, order, half, turn, out, total):
    s = pl.program_id(0)

    @pl.when(s == 0)
    def _():
        total[...] = jnp.zeros_like(total)

    total[...] += lax.dot_general(
        half[...], turn[...], (((1,), (1,)), ((), ())), preferred_element_type=jnp.float32
    )

    @pl.when(s == pl.num_programs(0) - 1)
    def _():
        share = out.shape[1]

        def device(d, carry):
            for r in range(share):
                out[d, r:r + 1, :] = total[pl.ds(order[d * share + r], 1), :] * scale
            return carry

        lax.fori_loop(0, out.shape[0], device, 0)


def product(devices, half_all, turn_all, order):
    rows, aux, orbitals = half_all.shape
    block = pl.BlockSpec((None, aux, orbitals), lambda s: (s, 0, 0))
    out = (devices, aux // devices, aux)
    return pl.pallas_call(
        functools.partial(product_kernel, 1.0 / orbitals),
        grid=(rows,),
        out_shape=jax.ShapeDtypeStruct(out, jnp.float32),
        in_specs=[pl.BlockSpec(memory_space=pltpu.SMEM), block, block],
        out_specs=pl.BlockSpec(out, lambda s: (0, 0, 0)),
        scratch_shapes=[pltpu.VMEM((aux, aux), jnp.float32)],
        compiler_params=pltpu.CompilerParams(vmem_limit_bytes=32 * MIB),
        cost_estimate=pl.CostEstimate(
            flops=2 * rows * aux * aux * orbitals,
            bytes_accessed=4 * rows * aux * orbitals, transcendentals=0,
        ),
    )(order, half_all, turn_all)


def sum_kernel(grp, pair, partial, out, arrived, send_sem, recv_sem):
    g, p = lax.axis_index("grp"), lax.axis_index("pair")
    devices = grp * pair
    me = g * pair + p
    enter(grp, pair)

    def copy(k):
        there = lax.rem(me + k, devices)
        return pltpu.make_async_remote_copy(
            src_ref=partial.at[there], dst_ref=arrived.at[me],
            send_sem=send_sem.at[k], recv_sem=recv_sem.at[me],
            device_id=(there // pair, lax.rem(there, pair)), device_id_type=MESH,
        )

    def start(k, carry):
        copy(k).start()
        return carry

    lax.fori_loop(1, devices, start, 0)
    out[...] = partial[me]

    def add(k, carry):
        sender = lax.rem(me + devices - k, devices)
        pltpu.make_async_remote_copy(
            src_ref=partial.at[sender], dst_ref=arrived.at[sender],
            send_sem=send_sem.at[k], recv_sem=recv_sem.at[sender],
            device_id=(sender // pair, lax.rem(sender, pair)), device_id_type=MESH,
        ).wait_recv()
        out[...] += arrived[sender]
        return carry

    lax.fori_loop(1, devices, add, 0)

    def sent(k, carry):
        copy(k).wait_send()
        return carry

    lax.fori_loop(1, devices, sent, 0)


def sum_shares(grp, pair, partial):
    devices, share, aux = partial.shape
    return pl.pallas_call(
        functools.partial(sum_kernel, grp, pair),
        out_shape=jax.ShapeDtypeStruct((share, aux), jnp.float32),
        in_specs=[pl.BlockSpec(memory_space=pltpu.VMEM)],
        out_specs=pl.BlockSpec(memory_space=pltpu.VMEM),
        scratch_shapes=[
            pltpu.VMEM((devices, share, aux), jnp.float32),
            pltpu.SemaphoreType.DMA((devices,)),
            pltpu.SemaphoreType.DMA((devices,)),
        ],
        compiler_params=pltpu.CompilerParams(
            collective_id=1, has_side_effects=True, vmem_limit_bytes=16 * MIB
        ),
    )(partial)


def density_own(density, mask_table, first):
    orbitals, cols = density.shape
    edge = orbitals // mask_table.shape[0]
    of = (first + jnp.arange(cols, dtype=jnp.int32)) // edge
    table = jnp.take(mask_table.T, of, axis=0).astype(density.dtype)
    return density.T * jnp.repeat(table, edge, axis=1)


def per_device(
    grp, pair,
    three_center, virt_density, occ_density, tensor_mask, virt_mask, occ_mask, panel_order,
):
    slab, width, orbitals = three_center.shape
    g, p = lax.axis_index("grp"), lax.axis_index("pair")
    cols = virt_density.shape[1]
    edge = orbitals // tensor_mask.shape[1]
    virt_own = density_own(virt_density, virt_mask, p * cols)
    occ_own = density_own(occ_density, occ_mask, p * cols)
    of = (p * slab + jnp.arange(slab, dtype=jnp.int32)) // edge
    table = lax.dynamic_slice_in_dim(tensor_mask, g * width // edge, width // edge, 1)
    mask = jnp.repeat(jnp.take(table, of, axis=0).astype(jnp.float32), edge, axis=2)
    half_all, turn_all = exchange(grp, pair, three_center, virt_own, occ_own, mask)
    partial = product(grp * pair, half_all, turn_all, panel_order)
    return sum_shares(grp, pair, partial)


def solution(mesh):
    placed = (P("pair", "grp", None), P(None, "pair"), P(None, "pair"), P(), P(), P(), P())
    sizes = mesh.shape["grp"], mesh.shape["pair"]
    return jax.shard_map(
        functools.partial(per_device, *sizes),
        mesh=mesh, in_specs=placed, out_specs=P(("grp", "pair"), None), check_vma=False,
    )
```

time: 2020 us -> 944 us (0.47)
  Pallas kernels: 0 us -> 926 us
  blocking collectives: 742 us -> 0 us
  waiting for transfers between devices: 634 us -> 0 us
  local copies, waits for them, and re-layouts: 427 us -> 8.53 us
  matrix products: 152 us -> 0 us
  other arithmetic: 26.7 us -> 1.17 us
    pallas_call x0 -> x3, Pallas kernels: none -> 926 us  [the longest x1 813 us: exchange(): pl.pallas_call(functools.partial(exchange_kernel, grp, pair, slots), out_...]
    all_to_all x1 -> x0, blocking collectives: 742 us -> none  [per_device(): lax.all_to_all(half, 'grp', split_axis=2, concat_axis=1, tiled=True)]
    all_to_all x2 -> x0, waiting for transfers between devices: 402 us -> none  [the longest x1 318 us: per_device(): lax.all_to_all(trans, 'pair', split_axis=2, concat_axis=0, tiled=True)]
    all_to_all x4 -> x0, local copies, waits for them, and re-layouts: 186 us -> none  [the longest x2 96 us: per_device(): lax.all_to_all(half, 'grp', split_axis=2, concat_axis=1, tiled=True)]
    dot_general x4 -> x0, matrix products: 152 us -> none  [the longest x1 61.5 us: per_device(): jnp.einsum('amn,ns->ams', masked, lax.all_gather(virt_local, 'pair', axis...]
    reduce_scatter x1 -> x0, waiting for transfers between devices: 132 us -> none  [per_device(): lax.psum_scatter(product_all, ('grp', 'pair'), scatter_dimension=0, tiled...]
    all_gather x2 -> x0, waiting for transfers between devices: 99.4 us -> none  [the longest x1 99.4 us: per_device(): lax.all_gather(occ_local, 'pair', axis=1, tiled=True)]
    convert_element_type x4 -> x0, local copies, waits for them, and re-layouts: 90.9 us -> none  [the longest x1 45.4 us: per_device(): trans = jnp.einsum('ams,ml->asl', swapped, lax.all_gather(occ_local, 'pai...]
  transfers between devices with their start and end apart: 5 -> 0, of which waited for: 4 -> 0; matrix products, arithmetic and copies ran while one was open for 12% -> 0% of each run, Pallas kernels for 0% -> 0%
where the time goes in v1:
time: 944 us; the launch traced here: 936 us
  Pallas kernels  926 us (98%)
    pallas_call x1, Pallas kernels, exchange(): pl.pallas_call(functools.partial(exchange_kernel, grp, pair, slots), out_...  813 us
    pallas_call x1, Pallas kernels, sum_shares(): pl.pallas_call(functools.partial(sum_kernel, grp, pair), out_shape=jax.Sh...  72.4 us
    pallas_call x1, Pallas kernels, product(): pl.pallas_call(functools.partial(product_kernel, 1.0 / orbitals), grid=(r...  40.7 us

profile of v1, /device:TPU:0, one launch (start us, length us, event | category | flops | bytes accessed | tf_op | source)
XLA Modules:
  0.0 936.2 jit_solution(9638983438956002786)
XLA Ops:
  0.0 0.0 copy-start
  0.1 0.6 copy-done
  0.7 0.8 copy.9
  1.5 0.8 copy.11
  2.2 0.7 gather_fusion
  2.9 0.1 select_convert_fusion.2
  3.0 0.6 gather_fusion.2
  3.7 0.6 gather_fusion.1
  4.3 0.1 select_convert_fusion
  4.4 0.2 broadcast_in_dim.29
  4.6 0.2 broadcast_in_dim.28
  4.8 1.1 copy.8
  5.9 1.1 copy.10
  7.0 0.9 bitcast_multiply_fusion
  7.9 0.2 broadcast_in_dim.32
  8.1 1.1 reshape.82.mask
  9.2 0.0 copy-start.2
  9.2 813.2 %shard_map.73 = (bf16[32,512,1024]{2,1,0:T(8,128)(2,1)}, bf16[32,512,1024]{2,1,0:T(8,128)(2,1)}) custom-call(bf16[64,256,1024]{2,1,0:T(8,128)(2,1)} %tensor.1, bf16[128,1024]{1,0:T(8,128)(2,1)} %get-tuple-element.13.virt_own, bf16[128,1024]{1,0:T(8,128)(2,1)} %get-tuple-element.12.occ_own, f32[64,2,1024]{2,1,0:T(2,128)} %reshape.82.mask), custom_call_target="tpu_custom_call" | custom-call | flops 68719476736 | bytes 100663296 | tf_op jit(solution)/shard_map/pallas_call | solution.py:242
  822.4 0.0 copy-start.1
  822.4 0.0 copy-done.2
  822.4 40.7 %shard_map.74.partial = f32[32,16,512]{2,1,0:T(8,128)S(1)} custom-call(s32[512]{0:T(512)S(1)} %copy-done.2, bf16[32,512,1024]{2,1,0:T(8,128)(2,1)} %get-tuple-element.8.half, bf16[32,512,1024]{2,1,0:T(8,128)(2,1)} %get-tuple-element.9.turn), custom_call_target="tpu_custom_call" | custom-call | flops 17179869184 | bytes 67108864 | tf_op jit(solution)/shard_map/pallas_call | solution.py:299
  863.1 72.4 %shard_map.75 = f32[16,512]{1,0:T(8,128)S(1)} custom-call(f32[32,16,512]{2,1,0:T(8,128)S(1)} %shard_map.74.partial), custom_call_target="tpu_custom_call" | custom-call | tf_op jit(solution)/shard_map/pallas_call | solution.py:356
  935.6 0.6 copy.17
  936.2 0.0 copy-done.1
  (7 shorter events, 0.1 us)
Async XLA Ops:
  0.0 0.7 copy-start
  9.2 813.3 %copy-start.2 = (s32[512]{0:T(512)S(1)}, s32[512]{0:T(512)}, u32[]{:S(2)}) copy-start(s32[512]{0:T(512)} %order.1) | copy-start | bytes 6148
  822.4 113.8 %copy-start.1 = (s32[4,8,8]{2,1,0:T(8,128)S(1)}, s32[4,8,8]{2,1,0:T(8,128)}, u32[]{:S(2)}) copy-start(s32[4,8,8]{2,1,0:T(8,128)} %param.12) | copy-start | bytes 3076

commit v2 on v0

v2 whole, which is shorter than its diff:
```python
import functools

import jax
import jax.numpy as jnp
from jax import lax
from jax.experimental import pallas as pl
from jax.experimental.pallas import tpu as pltpu
from jax.sharding import PartitionSpec as P

LANES = 128
MESH = pl.DeviceIdType.MESH
MIB = 1024 * 1024


def enter(grp, pair):
    g, p = lax.axis_index("grp"), lax.axis_index("pair")
    barrier = pltpu.get_barrier_semaphore()

    def greet(k, carry):
        there = lax.rem(g * pair + p + k, grp * pair)
        pl.semaphore_signal(
            barrier, inc=1, device_id=(there // pair, lax.rem(there, pair)), device_id_type=MESH
        )
        return carry

    lax.fori_loop(1, grp * pair, greet, 0)
    pl.semaphore_wait(barrier, grp * pair - 1)


def response_kernel(
    grp, pair, half_slots, turn_slots,
    tensor, virt_own, occ_own, mask, order,
    half_all, turn_all, out,
    tensor_buf, virt, occ, wide, half_buf, turn_buf, total, shares, arrived, column, crossed,
    load_sem, half_send, turn_send, half_recv, turn_recv, dens_send, dens_recv,
    share_send, share_recv, cross_send, cross_recv,
):
    g, p = lax.axis_index("grp"), lax.axis_index("pair")
    slab, width, orbitals = tensor.shape
    chunk = tensor_buf.shape[1]
    chunks = slab // chunk
    rows = width // pair
    cols = virt_own.shape[0]
    blocks = mask.shape[1]
    edge = width // blocks
    parts = width // LANES
    steps = parts * chunks * grp
    sibling = p + 1 - 2 * lax.rem(p, 2)

    def load(c):
        return pltpu.make_async_copy(
            tensor.at[pl.ds(lax.rem(c, chunks) * chunk, chunk)], tensor_buf.at[lax.rem(c, 2)],
            load_sem.at[lax.rem(c, 2)],
        )

    load(0).start()
    enter(grp, pair)

    def remote(src, dst, send_sem, recv_sem, to_grp, to_pair):
        return pltpu.make_async_remote_copy(
            src_ref=src, dst_ref=dst, send_sem=send_sem, recv_sem=recv_sem,
            device_id=(to_grp, to_pair), device_id_type=MESH,
        )

    def slab_of(which, q):
        return (virt, occ)[which].at[pl.ds(pl.multiple_of(q * cols, cols), cols)]

    def density(which, k):
        to = sibling if k == 0 else lax.rem(p + 2 * k, pair)
        return remote(
            (virt_own, occ_own)[which], slab_of(which, p),
            dens_send.at[which, k], dens_recv.at[which, p], g, to,
        )

    def density_in(which, q):
        part = slab_of(which, q)
        remote(part, part, dens_send.at[which, 0], dens_recv.at[which, q], g, sibling).wait_recv()

    def density_on(which, k):
        q = lax.rem(p + 2 * k, pair)
        part = slab_of(which, q)
        return remote(
            part, part, dens_send.at[which, pair // 2 + k], dens_recv.at[which, q], g, sibling
        )

    def pass_on(which):
        for k in range(1, pair // 2):
            density_in(which, lax.rem(p + 2 * k, pair))
            density_on(which, k).start()

    def rest_in(which):
        for k in range(pair // 2):
            density_in(which, lax.rem(sibling + 2 * k, pair))

    own_rows = pl.ds(pl.multiple_of(p * cols, cols), cols)
    for k in range(pair // 2):
        density(0, k).start()
    virt[own_rows, :] = virt_own[...]
    occ[own_rows, :] = occ_own[...]
    pass_on(0)
    for k in range(pair // 2):
        density(1, k).start()
    rest_in(0)

    def place(buf, slot):
        def one(s, carry):
            buf[slot, s] = wide[pl.ds(s, chunk, stride=width), :].astype(buf.dtype)
            return carry

        lax.fori_loop(0, width, one, 0, unroll=8)

    def keep(i, product):
        wide[pl.ds(pl.multiple_of(i * width, width), width), :] = product

    def wait_sent(buf, sems, slot):
        for k in range(pair):
            part = buf.at[slot, pl.ds(0, rows)]
            pltpu.make_async_copy(part, part, sems.at[slot, k]).wait()

    def send(buf, sends, slot, k, target_grp, dst, recv):
        target = lax.rem(p + k, pair)
        return remote(
            buf.at[slot, pl.ds(target * rows, rows)], dst, sends.at[slot, k], recv,
            target_grp, target,
        )

    def stay(buf, sends, slot, dst):
        return pltpu.make_async_copy(
            buf.at[slot, pl.ds(p * rows, rows)], dst, sends.at[slot, 0]
        )

    def step(t, carry):
        n, u = t // grp, lax.rem(t, grp)
        j, c = n // chunks, lax.rem(n, chunks)
        b = lax.rem(n, 2)
        half_slot, turn_slot = lax.rem(t, half_slots), lax.rem(t, turn_slots)

        @pl.when(u == 0)
        def _():
            load(n).wait()

            @pl.when(n + 1 < parts * chunks)
            def _():
                load(n + 1).start()

            def apply(i, carry):
                for block in range(blocks):
                    row = mask[c * chunk + i, block:block + 1, :]
                    row = jnp.broadcast_to(row, (16, orbitals)).astype(tensor_buf.dtype)
                    at = slice(block * edge, (block + 1) * edge)
                    part = tensor_buf[b, i, at, :].reshape(edge // 16, 16, orbitals)
                    tensor_buf[b, i, at, :] = (part * row[None]).reshape(edge, orbitals)
                return carry

            lax.fori_loop(0, chunk, apply, 0)

        @pl.when(t >= half_slots)
        def _():
            wait_sent(half_buf, half_send, half_slot)

        target_grp = lax.rem(g + 1 + u, grp)
        aux_rows = pl.ds(pl.multiple_of(p * slab + c * chunk, chunk), chunk)
        section = pl.ds(pl.multiple_of(j * LANES, LANES), LANES)

        def half_one(i, carry):
            left = virt[pl.ds(pl.multiple_of(target_grp * width, width), width), :]
            keep(i, lax.dot_general(
                left, tensor_buf[b, i, section, :], (((1,), (1,)), ((), ())),
                preferred_element_type=jnp.float32,
            ))
            return carry

        lax.fori_loop(0, chunk, half_one, 0)
        place(half_buf, half_slot)
        dst = half_all.at[j, :, aux_rows, pl.ds(pl.multiple_of(g * LANES, LANES), LANES)]
        recv = half_recv.at[j, g * pair + p]

        @pl.when(target_grp == g)
        def _():
            stay(half_buf, half_send, half_slot, dst).start()

        @pl.when(target_grp != g)
        def _():
            send(half_buf, half_send, half_slot, 0, target_grp, dst, recv).start()

        for k in range(1, pair):
            send(half_buf, half_send, half_slot, k, target_grp, dst, recv).start()

        @pl.when(t == 0)
        def _():
            pass_on(1)
            rest_in(1)

        @pl.when(t >= turn_slots)
        def _():
            wait_sent(turn_buf, turn_send, turn_slot)

        columns = pl.ds(pl.multiple_of(u * width + j * LANES, LANES), LANES)

        def turn_one(i, carry):
            keep(i, jnp.dot(
                tensor_buf[b, i], occ[:, columns], preferred_element_type=jnp.float32
            ))
            return carry

        lax.fori_loop(0, chunk, turn_one, 0)
        place(turn_buf, turn_slot)
        dst = turn_all.at[j, :, aux_rows, pl.ds(pl.multiple_of(u * LANES, LANES), LANES)]
        stay(turn_buf, turn_send, turn_slot, dst).start()
        for k in range(1, pair):
            send(turn_buf, turn_send, turn_slot, k, g, dst, turn_recv.at[j, p]).start()
        return carry

    lax.fori_loop(0, steps, step, 0)

    def all_in(j):
        def half_in(k, carry):
            sender = lax.rem(g * pair + p + k, grp * pair)
            sender_grp, sender_pair = sender // pair, lax.rem(sender, pair)
            part = half_all.at[
                j, :, pl.ds(pl.multiple_of(sender_pair * slab, slab), slab),
                pl.ds(pl.multiple_of(sender_grp * LANES, LANES), LANES),
            ]
            remote(
                part, part, half_send.at[0, 0], half_recv.at[j, sender], sender_grp, sender_pair
            ).wait_recv()
            return carry

        lax.fori_loop(1, grp * pair, half_in, 0)

        def turn_in(k, carry):
            sender = lax.rem(p + k, pair)
            part = turn_all.at[j, :, pl.ds(pl.multiple_of(sender * slab, slab), slab), :]
            remote(
                part, part, turn_send.at[0, 0], turn_recv.at[j, sender], g, sender
            ).wait_recv()
            return carry

        lax.fori_loop(1, pair, turn_in, 0)

    group = 4 if rows % 4 == 0 else 1
    aux = total.shape[0]

    def add_product(half, turn):
        value = total[...]
        for s in range(group):
            value += lax.dot_general(
                half[s], turn[s], (((1,), (1,)), ((), ())), preferred_element_type=jnp.float32
            )
        total[...] = value

    block = pl.BlockSpec((group, aux, grp * LANES), lambda s: (s, 0, 0))
    multiply = pltpu.emit_pipeline(add_product, grid=(rows // group,), in_specs=[block, block])

    total[...] = jnp.zeros_like(total)
    for j in range(parts):
        if j == parts - 1:
            for t in range(max(steps - half_slots, 0), steps):
                wait_sent(half_buf, half_send, t % half_slots)
            for t in range(max(steps - turn_slots, 0), steps):
                wait_sent(turn_buf, turn_send, t % turn_slots)
        all_in(j)
        multiply(half_all.at[j], turn_all.at[j])

    share = out.shape[0]

    def pick(d, carry):
        for r in range(share):
            row = total[pl.ds(order[d * share + r], 1), :]
            shares[lax.rem(d, pair), d // pair, r:r + 1, :] = row * (1.0 / orbitals)
        return carry

    lax.fori_loop(0, grp * pair, pick, 0)

    def over_pair(k):
        to = lax.rem(p + k, pair)
        return remote(shares.at[to], arrived.at[p], share_send.at[k], share_recv.at[p], g, to)

    for k in range(1, pair):
        over_pair(k).start()
    column[...] = shares[p]
    for k in range(1, pair):
        sender = lax.rem(p + pair - k, pair)
        part = arrived.at[sender]
        remote(part, part, share_send.at[k], share_recv.at[sender], g, sender).wait_recv()
        column[...] += arrived[sender]

    def over_grp(k):
        to = lax.rem(g + k, grp)
        return remote(column.at[to], crossed.at[g], cross_send.at[k], cross_recv.at[g], to, p)

    for k in range(1, grp):
        over_grp(k).start()
    out[...] = column[g]
    for k in range(1, grp):
        sender = lax.rem(g + grp - k, grp)
        part = crossed.at[sender]
        remote(part, part, cross_send.at[k], cross_recv.at[sender], sender, p).wait_recv()
        out[...] += crossed[sender]

    for k in range(1, grp):
        over_grp(k).wait_send()
    for k in range(1, pair):
        over_pair(k).wait_send()
    for which in range(2):
        for k in range(pair // 2):
            density(which, k).wait_send()
        for k in range(1, pair // 2):
            density_on(which, k).wait_send()


def response_share(grp, pair, tensor, virt_own, occ_own, mask, order):
    slab, width, orbitals = tensor.shape
    chunk = 16
    parts = width // LANES
    aux = slab * pair
    share = aux // (grp * pair)
    steps = parts * slab // chunk * grp
    half_slots, turn_slots = min(14, steps), min(8, steps)
    gathered = jax.ShapeDtypeStruct((parts, width // pair, aux, grp * LANES), tensor.dtype)
    kept = pltpu.VMEM
    dma = pltpu.SemaphoreType.DMA
    return pl.pallas_call(
        functools.partial(response_kernel, grp, pair, half_slots, turn_slots),
        out_shape=(gathered, gathered, jax.ShapeDtypeStruct((share, aux), jnp.float32)),
        in_specs=[pl.BlockSpec(memory_space=pl.ANY)]
        + [pl.BlockSpec(memory_space=kept)] * 3
        + [pl.BlockSpec(memory_space=pltpu.SMEM)],
        out_specs=(pl.BlockSpec(memory_space=pl.ANY),) * 2 + (pl.BlockSpec(memory_space=kept),),
        scratch_shapes=[
            kept((2, chunk, width, orbitals), tensor.dtype),
            kept((orbitals, orbitals), tensor.dtype),
            kept((orbitals, orbitals), tensor.dtype),
            kept((chunk * width, LANES), jnp.float32),
            kept((half_slots, width, chunk, LANES), tensor.dtype),
            kept((turn_slots, width, chunk, LANES), tensor.dtype),
            kept((aux, aux), jnp.float32),
            kept((pair, grp, share, aux), jnp.float32),
            kept((pair, grp, share, aux), jnp.float32),
            kept((grp, share, aux), jnp.float32),
            kept((grp, share, aux), jnp.float32),
            dma((2,)),
            dma((half_slots, pair)),
            dma((turn_slots, pair)),
            dma((parts, grp * pair)),
            dma((parts, pair)),
            dma((2, pair)),
            dma((2, pair)),
            dma((pair,)),
            dma((pair,)),
            dma((grp,)),
            dma((grp,)),
        ],
        compiler_params=pltpu.CompilerParams(
            collective_id=0, has_side_effects=True, vmem_limit_bytes=62 * MIB
        ),
        cost_estimate=pl.CostEstimate(
            flops=5 * slab * width * orbitals * orbitals,
            bytes_accessed=12 * slab * width * orbitals, transcendentals=0,
        ),
    )(tensor, virt_own, occ_own, mask, order)[2]


def density_own(density, mask_table, first):
    orbitals, cols = density.shape
    edge = orbitals // mask_table.shape[0]
    of = (first + jnp.arange(cols, dtype=jnp.int32)) // edge
    table = jnp.take(mask_table.T, of, axis=0).astype(density.dtype)
    return density.T * jnp.repeat(table, edge, axis=1)


def per_device(
    grp, pair,
    three_center, virt_density, occ_density, tensor_mask, virt_mask, occ_mask, panel_order,
):
    slab, width, orbitals = three_center.shape
    g, p = lax.axis_index("grp"), lax.axis_index("pair")
    cols = virt_density.shape[1]
    edge = orbitals // tensor_mask.shape[1]
    virt_own = density_own(virt_density, virt_mask, p * cols)
    occ_own = density_own(occ_density, occ_mask, p * cols)
    of = (p * slab + jnp.arange(slab, dtype=jnp.int32)) // edge
    table = lax.dynamic_slice_in_dim(tensor_mask, g * width // edge, width // edge, 1)
    mask = jnp.repeat(jnp.take(table, of, axis=0).astype(jnp.float32), edge, axis=2)
    return response_share(grp, pair, three_center, virt_own, occ_own, mask, panel_order)


def solution(mesh):
    placed = (P("pair", "grp", None), P(None, "pair"), P(None, "pair"), P(), P(), P(), P())
    sizes = mesh.shape["grp"], mesh.shape["pair"]
    return jax.shard_map(
        functools.partial(per_device, *sizes),
        mesh=mesh, in_specs=placed, out_specs=P(("grp", "pair"), None), check_vma=False,
    )
```

time: 2020 us -> 826 us (0.41)
  Pallas kernels: 0 us -> 815 us
  blocking collectives: 742 us -> 0 us
  waiting for transfers between devices: 634 us -> 0 us
  local copies, waits for them, and re-layouts: 427 us -> 9.3 us
  matrix products: 152 us -> 0 us
  other arithmetic: 26.7 us -> 1.18 us
    pallas_call x0 -> x1, Pallas kernels: none -> 815 us  [response_share(): pl.pallas_call(functools.partial(response_kernel, grp, pair, half_slots,...]
    all_to_all x1 -> x0, blocking collectives: 742 us -> none  [per_device(): lax.all_to_all(half, 'grp', split_axis=2, concat_axis=1, tiled=True)]
    all_to_all x2 -> x0, waiting for transfers between devices: 402 us -> none  [the longest x1 318 us: per_device(): lax.all_to_all(trans, 'pair', split_axis=2, concat_axis=0, tiled=True)]
    all_to_all x4 -> x0, local copies, waits for them, and re-layouts: 186 us -> none  [the longest x2 96 us: per_device(): lax.all_to_all(half, 'grp', split_axis=2, concat_axis=1, tiled=True)]
    dot_general x4 -> x0, matrix products: 152 us -> none  [the longest x1 61.5 us: per_device(): jnp.einsum('amn,ns->ams', masked, lax.all_gather(virt_local, 'pair', axis...]
    reduce_scatter x1 -> x0, waiting for transfers between devices: 132 us -> none  [per_device(): lax.psum_scatter(product_all, ('grp', 'pair'), scatter_dimension=0, tiled...]
    all_gather x2 -> x0, waiting for transfers between devices: 99.4 us -> none  [the longest x1 99.4 us: per_device(): lax.all_gather(occ_local, 'pair', axis=1, tiled=True)]
    convert_element_type x4 -> x0, local copies, waits for them, and re-layouts: 90.9 us -> none  [the longest x1 45.4 us: per_device(): trans = jnp.einsum('ams,ml->asl', swapped, lax.all_gather(occ_local, 'pai...]
  transfers between devices with their start and end apart: 5 -> 0, of which waited for: 4 -> 0; matrix products, arithmetic and copies ran while one was open for 12% -> 0% of each run, Pallas kernels for 0% -> 0%
where the time goes in v2:
time: 826 us; the launch traced here: 825 us
  Pallas kernels  815 us (99%)
  local copies, waits for them, and re-layouts  9.3 us (1%)
    pallas_call x1, Pallas kernels, response_share(): pl.pallas_call(functools.partial(response_kernel, grp, pair, half_slots,...  815 us

profile of v2, /device:TPU:0, one launch (start us, length us, event | category | flops | bytes accessed | tf_op | source)
XLA Modules:
  0.0 825.4 jit_solution(4074144452793170602)
XLA Ops:
  0.0 0.0 copy-start
  0.1 0.6 copy-done
  0.7 0.8 copy.9
  1.5 0.8 copy.11
  2.2 0.7 gather_fusion
  2.9 0.1 select_convert_fusion.2
  3.0 0.6 gather_fusion.2
  3.7 0.6 gather_fusion.1
  4.3 0.1 select_convert_fusion
  4.4 0.2 broadcast_in_dim.29
  4.6 0.2 broadcast_in_dim.28
  4.8 1.1 copy.8
  5.9 1.1 copy.10
  7.0 0.9 bitcast_multiply_fusion
  7.9 0.2 broadcast_in_dim.32
  8.1 1.1 reshape.82.mask
  9.2 0.0 copy-start.1
  9.2 814.8 %shard_map.73 = (bf16[2,32,512,512]{3,2,1,0:T(8,128)(2,1)}, bf16[2,32,512,512]{3,2,1,0:T(8,128)(2,1)}, f32[16,512]{1,0:T(8,128)}) custom-call(bf16[64,256,1024]{2,1,0:T(8,128)(2,1)} %tensor.1, bf16[128,1024]{1,0:T(8,128)(2,1)} %get-tuple-element.11.virt_own, bf16[128,1024]{1,0:T(8,128)(2,1)} %get-tuple-element.10.occ_own, f32[64,2,1024]{2,1,0:T(2,128)} %reshape.82.mask, ...), custom_call_target="tpu_custom_call" | custom-call | flops 85899345920 | bytes 201326592 | tf_op jit(solution)/shard_map/pallas_call | solution.py:323
  824.0 1.4 copy.17
  825.4 0.0 copy-done.1
  (7 shorter events, 0.1 us)
Async XLA Ops:
  0.0 0.7 copy-start
  9.2 816.2 %copy-start.1 = (s32[4,8,8]{2,1,0:T(8,128)S(1)}, s32[4,8,8]{2,1,0:T(8,128)}, u32[]{:S(2)}) copy-start(s32[4,8,8]{2,1,0:T(8,128)} %param.12) | copy-start | bytes 3076
